TPU v7x, 32 devices: a whole 2x2x4 slice. The times are simulated.
32 devices in a mesh: grp: 2 (over y), pencil: 4 (over z), depth: 2 (over x), mem: 2 (over core).
Axes of the slice: x: 2, y: 2, z: 4, core: 2. Of those that a mesh axis runs over, the one named last changes fastest.
Arguments:
- density: float32 [4, 2, 2048, 2048], P(('grp', 'mem'), 'depth', 'pencil'), parts along dimension 0, may hold values from -6 to 6
- background: float32 [8, 2], P(None, 'depth'), may hold values from -2 to 2
- member_ids: int32 [4], P(('grp', 'mem')), parts along dimension 0, may hold values from 0 to 7
- layer_kernel: int32 [2], P('depth'), may hold values from 0 to 3, as said below
- kernel_spectra: bfloat16 [4, 2, 2048, 2048], P('depth', None, None, 'pencil'), may hold values from -4 to 4
Outputs:
- gravity: float32 [4, 2048, 2048], P(('grp', 'mem'), ('pencil', 'depth')), parts along dimension 0
There are 2 independent parts, one for each index of `grp`. A program takes and returns all parts, laid end to end along the dimension named above; an argument that names none is the same for every part. Nothing has to cross between parts.
Inputs may be any that keep to these rules, and one draw needn't show every extreme that they name: Layer l takes one of the 2 kernels of its depth band: layer_kernel[l] // 2 equals l.
All inputs are finite; a program needn't handle non-finite values.
Results may differ from a plain program's by a relative error of at most 0.0003.
Values sent between devices are 32-bit elements; how exact they have to be, the bound alone decides.
A program may use at most 128 MiB of HBM per device.

v0:
```python
import math
import jax
import jax.numpy as jnp
from jax import lax
from jax.sharding import PartitionSpec as P

base_radix = 16
highest = lax.Precision.HIGHEST


def twiddle_table(row_count, col_count, modulus):
    left_index = lax.broadcasted_iota(jnp.int32, (row_count, col_count), 0)
    right_index = lax.broadcasted_iota(jnp.int32, (row_count, col_count), 1)
    angles = (left_index * right_index % modulus).astype(jnp.float32) * (2.0 * math.pi / modulus)
    return (jnp.cos(angles), jnp.sin(angles))


def forward_rows(values):
    leading = values.shape[:-1]
    length = values.shape[-1]
    inner_len = length // base_radix
    blocks = values.reshape(leading + (base_radix, inner_len))
    cos_small, sin_small = twiddle_table(base_radix, base_radix, base_radix)
    first_real = jnp.einsum("kn,...nm->...km", cos_small, blocks, precision=highest)
    first_imag = -jnp.einsum("kn,...nm->...km", sin_small, blocks, precision=highest)
    cos_turn, sin_turn = twiddle_table(base_radix, inner_len, length)
    turned_real = first_real * cos_turn + first_imag * sin_turn
    turned_imag = first_imag * cos_turn - first_real * sin_turn
    cos_large, sin_large = twiddle_table(inner_len, inner_len, inner_len)
    final_real = jnp.einsum(
        "...kn,nm->...km", turned_real, cos_large, precision=highest
    ) + jnp.einsum("...kn,nm->...km", turned_imag, sin_large, precision=highest)
    final_imag = jnp.einsum(
        "...kn,nm->...km", turned_imag, cos_large, precision=highest
    ) - jnp.einsum("...kn,nm->...km", turned_real, sin_large, precision=highest)
    return (final_real.reshape(leading + (length,)), final_imag.reshape(leading + (length,)))


def forward_columns(real_part, imag_part):
    leading = real_part.shape[:-2]
    length = real_part.shape[-2]
    col_width = real_part.shape[-1]
    inner_len = length // base_radix
    block_shape = leading + (base_radix, inner_len, col_width)
    split_real = real_part.reshape(block_shape)
    split_imag = imag_part.reshape(block_shape)
    cos_small, sin_small = twiddle_table(base_radix, base_radix, base_radix)
    first_real = jnp.einsum(
        "kn,...nmq->...kmq", cos_small, split_real, precision=highest
    ) + jnp.einsum("kn,...nmq->...kmq", sin_small, split_imag, precision=highest)
    first_imag = jnp.einsum(
        "kn,...nmq->...kmq", cos_small, split_imag, precision=highest
    ) - jnp.einsum("kn,...nmq->...kmq", sin_small, split_real, precision=highest)
    cos_turn, sin_turn = twiddle_table(base_radix, inner_len, length)
    cos_turn = cos_turn[:, :, None]
    sin_turn = sin_turn[:, :, None]
    turned_real = first_real * cos_turn + first_imag * sin_turn
    turned_imag = first_imag * cos_turn - first_real * sin_turn
    cos_large, sin_large = twiddle_table(inner_len, inner_len, inner_len)
    final_real = jnp.einsum(
        "...kmq,mj->...kjq", turned_real, cos_large, precision=highest
    ) + jnp.einsum("...kmq,mj->...kjq", turned_imag, sin_large, precision=highest)
    final_imag = jnp.einsum(
        "...kmq,mj->...kjq", turned_imag, cos_large, precision=highest
    ) - jnp.einsum("...kmq,mj->...kjq", turned_real, sin_large, precision=highest)
    out_shape = leading + (length, col_width)
    return (final_real.reshape(out_shape), final_imag.reshape(out_shape))


def inverse_columns(real_part, imag_part):
    length = real_part.shape[0]
    col_width = real_part.shape[1]
    inner_len = length // base_radix
    split_real = real_part.reshape(base_radix, inner_len, col_width)
    split_imag = imag_part.reshape(base_radix, inner_len, col_width)
    cos_large, sin_large = twiddle_table(inner_len, inner_len, inner_len)
    first_real = jnp.einsum("kmq,mj->kjq", split_real, cos_large, precision=highest) - jnp.einsum(
        "kmq,mj->kjq", split_imag, sin_large, precision=highest
    )
    first_imag = jnp.einsum("kmq,mj->kjq", split_imag, cos_large, precision=highest) + jnp.einsum(
        "kmq,mj->kjq", split_real, sin_large, precision=highest
    )
    cos_turn, sin_turn = twiddle_table(base_radix, inner_len, length)
    cos_turn = cos_turn[:, :, None]
    sin_turn = sin_turn[:, :, None]
    turned_real = first_real * cos_turn - first_imag * sin_turn
    turned_imag = first_imag * cos_turn + first_real * sin_turn
    cos_small, sin_small = twiddle_table(base_radix, base_radix, base_radix)
    final_real = jnp.einsum("nk,kjq->njq", cos_small, turned_real, precision=highest) - jnp.einsum(
        "nk,kjq->njq", sin_small, turned_imag, precision=highest
    )
    final_imag = jnp.einsum("nk,kjq->njq", cos_small, turned_imag, precision=highest) + jnp.einsum(
        "nk,kjq->njq", sin_small, turned_real, precision=highest
    )
    return (final_real.reshape(length, col_width), final_imag.reshape(length, col_width))


def inverse_rows(real_part, imag_part):
    row_count = real_part.shape[0]
    length = real_part.shape[1]
    inner_len = length // base_radix
    split_real = real_part.reshape(row_count, base_radix, inner_len)
    split_imag = imag_part.reshape(row_count, base_radix, inner_len)
    cos_large, sin_large = twiddle_table(inner_len, inner_len, inner_len)
    first_real = jnp.einsum("rkm,mj->rkj", split_real, cos_large, precision=highest) - jnp.einsum(
        "rkm,mj->rkj", split_imag, sin_large, precision=highest
    )
    first_imag = jnp.einsum("rkm,mj->rkj", split_imag, cos_large, precision=highest) + jnp.einsum(
        "rkm,mj->rkj", split_real, sin_large, precision=highest
    )
    cos_turn, sin_turn = twiddle_table(base_radix, inner_len, length)
    turned_real = first_real * cos_turn - first_imag * sin_turn
    turned_imag = first_imag * cos_turn + first_real * sin_turn
    cos_small, sin_small = twiddle_table(base_radix, base_radix, base_radix)
    final_real = jnp.einsum("nk,rkj->rnj", cos_small, turned_real, precision=highest) - jnp.einsum(
        "nk,rkj->rnj", sin_small, turned_imag, precision=highest
    )
    return final_real.reshape(row_count, length)


def body(density, background, member_ids, layer_kernel, kernel_spectra):
    profiles = background.shape[0]
    chosen = (lax.broadcasted_iota(jnp.int32, (profiles,), 0) == member_ids[0]).astype(jnp.float32)
    offsets = jnp.dot(chosen, background, precision=highest)
    contrast = density[0] - offsets[:, None, None]
    row_real, row_imag = forward_rows(contrast)
    paired = jnp.stack([row_real, row_imag], axis=1)
    layer_block = lax.all_to_all(paired, "pencil", split_axis=3, concat_axis=2, tiled=True)
    out_real, out_imag = forward_columns(layer_block[:, 0], layer_block[:, 1])
    spectra = jnp.stack([out_real, out_imag], axis=1)
    kern_count = kernel_spectra.shape[0]
    layer_count = layer_kernel.shape[0]
    band_start = lax.axis_index("depth") * kern_count
    local_index = layer_kernel - band_start
    weights = (
        local_index[:, None] == lax.broadcasted_iota(jnp.int32, (layer_count, kern_count), 1)
    ).astype(jnp.float32)
    binned = jnp.einsum("lk,lcxq->kcxq", weights, spectra, precision=highest)
    kernels = kernel_spectra.astype(jnp.float32)
    part_real = jnp.sum(binned[:, 0] * kernels[:, 0] - binned[:, 1] * kernels[:, 1], axis=0)
    part_imag = jnp.sum(binned[:, 0] * kernels[:, 1] + binned[:, 1] * kernels[:, 0], axis=0)
    partial_value = jnp.stack([part_real, part_imag], axis=0)
    depth_count = lax.axis_size("depth")
    pencil_count = lax.axis_size("pencil")
    length_x = partial_value.shape[1]
    col_width = partial_value.shape[2]
    rows_out = length_x // (pencil_count * depth_count)
    summed = lax.psum(partial_value, "depth")
    field_real, field_imag = inverse_columns(summed[0], summed[1])
    stacked = jnp.stack([field_real, field_imag], axis=1)
    own_rows = lax.dynamic_index_in_dim(
        stacked.reshape(pencil_count, depth_count, rows_out, 2, col_width),
        lax.axis_index("depth"),
        1,
        keepdims=False,
    )
    gathered = lax.all_to_all(own_rows, "pencil", split_axis=0, concat_axis=3, tiled=True)
    grid_rows = gathered[0]
    result = inverse_rows(grid_rows[:, 0], grid_rows[:, 1]) * (
        1.0 / (length_x * grid_rows.shape[-1])
    )
    return result[None]


def solution(mesh):
    placed = (
        P(("grp", "mem"), "depth", "pencil", None),
        P(None, "depth"),
        P(("grp", "mem")),
        P("depth"),
        P("depth", None, None, "pencil"),
    )
    return jax.shard_map(
        body,
        mesh=mesh,
        in_specs=placed,
        out_specs=P(("grp", "mem"), ("pencil", "depth"), None),
        check_vma=False,
    )
```

profile of v0, /device:TPU:0, one launch (start us, length us, event | category | flops | bytes accessed | tf_op | source)
XLA Modules:
  0.0 762.8 jit_solution(689112349098130173)
XLA Ops:
  16.6 4.8 fusion.8
  21.4 5.9 fusion.35
  27.3 5.7 fusion.37
  32.9 6.1 fusion.43
  39.0 5.8 fusion.46
  44.8 8.0 %copy.122 = f32[1,1,512,2048]{2,1,0,3:T(1,128)S(1)} copy(f32[1,1,512,2048]{2,3,1,0:T(8,128)S(1)} %bitcast.222) | data formatting | bytes 8388608 | tf_op jit(solution)/shard_map/stack;reshape | solution.py:127
  52.8 8.0 %copy.121 = f32[1,1,512,2048]{2,1,0,3:T(1,128)S(1)} copy(f32[1,1,512,2048]{2,3,1,0:T(8,128)S(1)} %bitcast.221) | data formatting | bytes 8388608 | tf_op jit(solution)/shard_map/stack;reshape | solution.py:127
  60.8 8.8 %pad_maximum_fusion = f32[1,2,512,2048]{2,1,0,3:T(2,128)} fusion(f32[1,1,512,2048]{2,1,0,3:T(1,128)S(1)} %copy.122, f32[1,1,512,2048]{2,1,0,3:T(1,128)S(1)} %copy.121), kind=kLoop, calls=%fused_computation | loop fusion | flops 2097152 | bytes 16777216 | tf_op jit(solution)/shard_map/stack | solution.py:127
  69.6 6.3 all-to-all-start
  76.8 11.5 %convert_element_type.136 = f32[2,2,2048,512]{3,2,1,0:T(8,128)} convert(bf16[2,2,2048,512]{3,2,1,0:T(8,128)(2,1)} %param.9) | non-fusion elementwise | flops 4194304 | bytes 25165824 | tf_op jit(solution)/shard_map/convert_element_type | solution.py:139
  88.3 171.7 %all-to-all-done = f32[1,2,512,2048]{2,1,0,3:T(2,128)} async-done(((f32[1,2,512,2048]{2,1,0,3:T(2,128)}), f32[1,2,512,2048]{2,1,0,3:T(2,128)}, u32[]{:S(2)}, u32[]{:S(2)}) %all-to-all-start) | async-done | bytes 8388640 | tf_op jit(solution)/shard_map/all_to_all | solution.py:128
  260.0 8.2 %copy.123 = f32[1,2,512,2048]{2,3,1,0:T(8,128)} copy(f32[1,2,512,2048]{2,1,0,3:T(2,128)} %all-to-all-done) | data formatting | bytes 16777216 | tf_op jit(solution)/shard_map/all_to_all | solution.py:128
  268.2 10.0 %copy.124 = f32[1,2,4,512,512]{4,3,2,1,0:T(8,128)} copy(f32[1,2,4,512,512]{3,4,2,1,0:T(8,128)} %bitcast.216) | data formatting | bytes 16777216 | tf_op jit(solution)/shard_map/all_to_all | solution.py:128
  282.7 6.8 fusion.27
  289.5 6.8 fusion.29
  296.3 7.2 fusion.49
  303.5 8.9 %fusion.4 = (f32[16,128,512]{2,0,1:T(8,128)S(1)}, f32[16,128,512]{2,0,1:T(8,128)S(1)}) fusion(f32[128,512,16]{1,2,0:T(8,128)S(1)} %fusion.49, f32[16,128]{0,1:T(8,128)S(1)} %copy.130, f32[16,128]{0,1:T(8,128)S(1)} %copy.127, f32[128,512,16]{1,2,0:T(8,128)S(1)} %fusion.27, f32[16,128,512]{2,1,0:T(8,128)S(1)} %bitcast.206), kind=kOutput, calls=%fused_computation.18 | convolution fusion | flops 208670208 | bytes 20987904 | tf_op jit(solution)/shard_map/kn,...nmq->...kmq/dot_general | solution.py:53
  312.4 6.1 fusion.19
  318.5 6.5 fusion.21
  325.1 6.4 fusion.55
  331.5 6.7 fusion.58
  342.4 11.4 %broadcast_multiply_fusion = f32[2,2,2048,512]{3,2,1,0:T(8,128)} fusion(f32[2,2048,512]{2,1,0:T(8,128)} %maximum_bitcast_fusion, f32[2]{0:T(128)S(1)} %fusion.159), kind=kLoop, calls=%fused_computation.7 | loop fusion | flops 4194304 | bytes 25165832 | tf_op jit(solution)/shard_map/lk,lcxq->kcxq/dot_general | solution.py:138
  353.8 17.3 %subtract_reduce_fusion = (f32[2048,512]{1,0:T(8,128)}, f32[2048,512]{1,0:T(8,128)}) fusion(f32[2,2,2048,512]{3,2,1,0:T(8,128)} %convert_element_type.136, f32[2,2,2048,512]{3,2,1,0:T(8,128)} %broadcast_multiply_fusion), kind=kLoop, calls=%fused_computation.6 | loop fusion | flops 14680064 | bytes 41943040 | tf_op jit(solution)/shard_map/reduce_sum | solution.py:140
  371.1 7.7 %pad_maximum_fusion.1 = f32[2,2048,512]{2,1,0:T(8,128)} fusion(f32[1,2048,512]{2,1,0:T(8,128)} %bitcast.225, f32[1,2048,512]{2,1,0:T(8,128)} %bitcast.224), kind=kLoop, calls=%fused_computation.2 | loop fusion | flops 2097152 | bytes 16777216 | tf_op jit(solution)/shard_map/stack | solution.py:142
  378.8 197.3 %all-reduce.2.cloned.1.call-done = f32[2,2048,512]{2,1,0:T(8,128)} async-done(((f32[2,2048,512]{2,1,0:T(8,128)}), f32[2,2048,512]{2,1,0:T(8,128)}) %all-reduce.2.cloned.1.call-update) | async-done | bytes 8388624 | tf_op jit(solution)/shard_map/psum | solution.py:148
  593.5 5.3 fusion.1
  598.9 6.0 fusion.11
  604.9 5.6 fusion.13
  610.5 6.1 fusion.61
  616.6 5.7 fusion.64
  627.8 97.6 %all_to_all.33 = f32[4,256,2,512]{3,1,2,0:T(8,128)} all-to-all(f32[4,256,2,512]{3,1,2,0:T(8,128)S(1)} %copy_bitcast_fusion), channel_id=1, replica_groups=mesh['grp'=2,'pencil'=4,'depth'=2,'mem'=2] {'pencil'}, dimensions={0} | all-to-all | bytes 8388608 | tf_op jit(solution)/shard_map/all_to_all | solution.py:157
  725.4 5.2 copy.150
  (27 shorter events, 66.1 us)
Async XLA Ops:
  69.6 190.4 %all-to-all-start = ((f32[1,2,512,2048]{2,1,0,3:T(2,128)}), f32[1,2,512,2048]{2,1,0,3:T(2,128)}, u32[]{:S(2)}, u32[]{:S(2)}) async-start(f32[1,2,512,2048]{2,1,0,3:T(2,128)} %pad_maximum_fusion), calls=%async_computation | async-start | bytes 16777216 | tf_op jit(solution)/shard_map/all_to_all | solution.py:128
  75.9 500.2 %all-reduce.2.cloned.1.call-start = ((), (), s32[]{:S(2)}) async-start(), calls=%async_computation.2 | async-start | bytes 16777216 | tf_op jit(solution)/shard_map/psum | solution.py:148
Sparse Core Ops, SparseCore 0:
  378.9 197.1 all-reduce.1
where the time goes:
time: 772 us; the launch traced here: 763 us
  waiting for transfers between devices  369 us (48%)
  matrix products  150 us (19%)
  blocking collectives  97.6 us (13%)
  other arithmetic  66 us (9%)
  local copies, waits for them, and re-layouts  58.4 us (8%)
  between operations  15.2 us (2%)
    psum x1, waiting for transfers between devices, body(): summed = lax.psum(partial_value, 'depth')  197 us
    all_to_all x1, waiting for transfers between devices, body(): lax.all_to_all(paired, 'pencil', split_axis=3, concat_axis=2, tiled=True)  172 us
    all_to_all x1, blocking collectives, body(): lax.all_to_all(own_rows, 'pencil', split_axis=0, concat_axis=3, tiled=True)  97.6 us
    all_to_all x2, local copies, waits for them, and re-layouts, body(): lax.all_to_all(paired, 'pencil', split_axis=3, concat_axis=2, tiled=True)  18.2 us
    reduce_sum x1, other arithmetic, body(): jnp.sum(binned[:, 0] * kernels[:, 0] - binned[:, 1] * kernels[:, 1], axis=0)  17.3 us
    another operation x2, local copies, waits for them, and re-layouts, body(): paired = jnp.stack([row_real, row_imag], axis=1)  16 us
  transfers between devices with their start and end apart: 2, of which 2 were waited for; matrix products, arithmetic and copies ran while one was open for 2% of the time, Pallas kernels for 0%

commit v1 on v0

--- a/solution.py
+++ b/solution.py
@@ -3,9 +3,21 @@
 import jax.numpy as jnp
 from jax import lax
 from jax.sharding import PartitionSpec as P
+from jax.lax import axis_index, ppermute, psum
 
 base_radix = 16
 highest = lax.Precision.HIGHEST
+
+
+def link_joints(block_in, dim_k, local_array):
+    opened, finding = (block_in.shape[:dim_k], block_in.shape[dim_k + 1 :])
+    return jnp.moveaxis(block_in.reshape(*opened, local_array, -1, *finding), dim_k, 0)
+
+
+def check_space(incoming_x, d0):
+    x_now = list(incoming_x.shape[1:])
+    x_now[d0] *= incoming_x.shape[0]
+    return jnp.moveaxis(incoming_x, 0, d0).reshape(x_now)
 
 
 def twiddle_table(row_count, col_count, modulus):
@@ -125,7 +137,14 @@
     contrast = density[0] - offsets[:, None, None]
     row_real, row_imag = forward_rows(contrast)
     paired = jnp.stack([row_real, row_imag], axis=1)
-    layer_block = lax.all_to_all(paired, "pencil", split_axis=3, concat_axis=2, tiled=True)
+    clean, u_next = (psum(1, "pencil"), axis_index("pencil"))
+    newest = link_joints(paired, 3, clean)
+    stack_in = [newest[u_next]]
+    for num in range(1, clean):
+        work_now = newest[u_next ^ num]
+        stack_in.append(ppermute(work_now, "pencil", [(t, t ^ num) for t in range(clean)]))
+    newest = jnp.stack(stack_in, axis=0)[u_next ^ jnp.arange(clean)]
+    layer_block = check_space(newest, 2)
     out_real, out_imag = forward_columns(layer_block[:, 0], layer_block[:, 1])
     spectra = jnp.stack([out_real, out_imag], axis=1)
     kern_count = kernel_spectra.shape[0]

time: 772 us -> 752 us (0.974)
  local copies, waits for them, and re-layouts: 58.4 us -> 43.3 us
  waiting for transfers between devices: 369 us -> 358 us
    all_to_all x1 -> x0, waiting for transfers between devices: 172 us -> none  [body(): lax.all_to_all(paired, 'pencil', split_axis=3, concat_axis=2, tiled=True)]
    ppermute x0 -> x3, waiting for transfers between devices: none -> 159 us  [body(): ppermute(work_now, 'pencil', [(t, t ^ num) for t in range(clean)])]
    all_to_all x2 -> x0, local copies, waits for them, and re-layouts: 18.2 us -> none  [body(): lax.all_to_all(paired, 'pencil', split_axis=3, concat_axis=2, tiled=True)]
    another operation x2 -> x4, local copies, waits for them, and re-layouts: 16 us -> 10.5 us  [body(): paired = jnp.stack([row_real, row_imag], axis=1)]
  transfers between devices with their start and end apart: 2 -> 4, of which waited for: 2 -> 3; matrix products, arithmetic and copies ran while one was open for 2% -> 3% of each run, Pallas kernels for 0% -> 0%
where the time goes in v1:
time: 752 us; the launch traced here: 743 us
  waiting for transfers between devices  358 us (48%)
  matrix products  154 us (20%)
  blocking collectives  97.6 us (13%)
  other arithmetic  69.4 us (9%)
  local copies, waits for them, and re-layouts  43.3 us (6%)
  between operations  15.4 us (2%)
    psum x1, waiting for transfers between devices, body(): summed = lax.psum(partial_value, 'depth')  198 us
    ppermute x3, waiting for transfers between devices, body(): ppermute(work_now, 'pencil', [(t, t ^ num) for t in range(clean)])  159 us
    all_to_all x1, blocking collectives, body(): lax.all_to_all(own_rows, 'pencil', split_axis=0, concat_axis=3, tiled=True)  97.6 us
    reduce_sum x1, other arithmetic, body(): jnp.sum(binned[:, 0] * kernels[:, 0] - binned[:, 1] * kernels[:, 1], axis=0)  17.1 us
  transfers between devices with their start and end apart: 4, of which 3 were waited for; matrix products, arithmetic and copies ran while one was open for 3% of the time, Pallas kernels for 0%

profile of v1, /device:TPU:0, one launch (start us, length us, event | category | flops | bytes accessed | tf_op | source)
XLA Modules:
  0.0 742.7 jit_solution(319729114763775752)
XLA Ops:
  16.4 4.8 fusion.8
  21.2 5.9 fusion.35
  27.1 5.5 fusion.37
  32.6 7.8 %fusion.43 = f32[512,16,128]{0,2,1:T(8,128)} fusion(f32[512,16,128]{0,2,1:T(8,128)S(1)} %fusion.37, f32[512,16,128]{2,1,0:T(8,128)S(1)} %get-tuple-element.11), kind=kOutput, calls=%fused_computation.74 | convolution fusion | flops 1611890688 | bytes 12582912 | tf_op jit(solution)/shard_map/...kn,nm->...km/dot_general | solution.py:42
  40.4 7.5 %fusion.46 = f32[512,16,128]{0,2,1:T(8,128)} fusion(f32[512,16,128]{0,2,1:T(8,128)S(1)} %fusion.35, f32[512,16,128]{2,1,0:T(8,128)S(1)} %get-tuple-element.11), kind=kOutput, calls=%fused_computation.75 | convolution fusion | flops 1611890688 | bytes 12582912 | tf_op jit(solution)/shard_map/...kn,nm->...km/dot_general | solution.py:47
  48.0 6.7 fusion.68
  57.6 5.1 collective-permute-start.2
  71.7 11.6 %convert_element_type.136 = f32[2,2,2048,512]{3,2,1,0:T(8,128)} convert(bf16[2,2,2048,512]{3,2,1,0:T(8,128)(2,1)} %param.9) | non-fusion elementwise | flops 4194304 | bytes 25165824 | tf_op jit(solution)/shard_map/convert_element_type | solution.py:158
  83.4 26.2 %collective-permute-done.2 = f32[1,2,512,512]{3,2,1,0:T(8,128)} collective-permute-done((f32[1,2,512,512]{3,2,1,0:T(8,128)}, f32[1,2,512,512]{3,2,1,0:T(8,128)}, u32[]{:S(2)}, u32[]{:S(2)}) %collective-permute-start.2) | collective-permute-done | bytes 2097184 | tf_op jit(solution)/shard_map/ppermute | solution.py:145
  109.6 133.0 %collective-permute-done.1 = f32[1,2,512,512]{3,2,1,0:T(8,128)} collective-permute-done((f32[1,2,512,512]{3,2,1,0:T(8,128)}, f32[1,2,512,512]{3,2,1,0:T(8,128)}, u32[]{:S(2)}, u32[]{:S(2)}) %collective-permute-start.1) | collective-permute-done | bytes 2097184 | tf_op jit(solution)/shard_map/ppermute | solution.py:145
  242.6 5.7 maximum_bitcast_fusion
  248.3 7.7 %gather_fusion = f32[4,2,512,512]{3,2,1,0:T(8,128)} fusion(f32[4,2,512,512]{3,2,1,0:T(8,128)} %maximum_bitcast_fusion, s32[1024]{0:T(1024)S(1)} %pad_clamp_fusion), kind=kCustom, calls=%fused_computation | custom fusion | bytes 16777232 | tf_op jit(solution)/shard_map/gather | solution.py:146
  261.4 6.8 fusion.27
  268.2 6.8 fusion.29
  275.0 7.2 fusion.49
  282.2 8.9 %fusion.4 = (f32[16,128,512]{2,0,1:T(8,128)S(1)}, f32[16,128,512]{2,0,1:T(8,128)S(1)}) fusion(f32[128,512,16]{1,2,0:T(8,128)S(1)} %fusion.49, f32[16,128]{0,1:T(8,128)S(1)} %copy.90, f32[16,128]{0,1:T(8,128)S(1)} %copy.87, f32[128,512,16]{1,2,0:T(8,128)S(1)} %fusion.27, f32[16,128,512]{2,1,0:T(8,128)S(1)} %bitcast.217), kind=kOutput, calls=%fused_computation.27 | convolution fusion | flops 208670208 | bytes 20987904 | tf_op jit(solution)/shard_map/kn,...nmq->...kmq/dot_general | solution.py:65
  291.1 6.3 fusion.19
  297.4 6.3 fusion.21
  303.7 6.8 fusion.55
  310.6 6.5 fusion.58
  321.3 11.4 %broadcast_multiply_fusion = f32[2,2,2048,512]{3,2,1,0:T(8,128)} fusion(f32[2,2048,512]{2,1,0:T(8,128)} %maximum_bitcast_fusion.1, f32[2]{0:T(128)S(1)} %fusion.191), kind=kLoop, calls=%fused_computation.16 | loop fusion | flops 4194304 | bytes 25165832 | tf_op jit(solution)/shard_map/lk,lcxq->kcxq/dot_general | solution.py:157
  332.7 17.1 %subtract_reduce_fusion = (f32[2048,512]{1,0:T(8,128)}, f32[2048,512]{1,0:T(8,128)}) fusion(f32[2,2,2048,512]{3,2,1,0:T(8,128)} %convert_element_type.136, f32[2,2,2048,512]{3,2,1,0:T(8,128)} %broadcast_multiply_fusion), kind=kLoop, calls=%fused_computation.15 | loop fusion | flops 14680064 | bytes 41943040 | tf_op jit(solution)/shard_map/reduce_sum | solution.py:159
  349.8 7.7 %pad_maximum_fusion = f32[2,2048,512]{2,1,0:T(8,128)} fusion(f32[1,2048,512]{2,1,0:T(8,128)} %bitcast.236, f32[1,2048,512]{2,1,0:T(8,128)} %bitcast.235), kind=kLoop, calls=%fused_computation.11 | loop fusion | flops 2097152 | bytes 16777216 | tf_op jit(solution)/shard_map/stack | solution.py:161
  357.5 198.3 %all-reduce.2.cloned.1.call-done = f32[2,2048,512]{2,1,0:T(8,128)} async-done(((f32[2,2048,512]{2,1,0:T(8,128)}), f32[2,2048,512]{2,1,0:T(8,128)}) %all-reduce.2.cloned.1.call-update) | async-done | bytes 8388624 | tf_op jit(solution)/shard_map/psum | solution.py:167
  568.6 4.6 convolution_subtract_fusion
  573.2 5.3 fusion.1
  578.5 6.2 fusion.11
  584.7 5.6 fusion.13
  590.3 5.8 fusion.61
  596.1 5.7 fusion.64
  607.4 97.6 %all_to_all.15 = f32[4,256,2,512]{3,1,2,0:T(8,128)} all-to-all(f32[4,256,2,512]{3,1,2,0:T(8,128)S(1)} %copy_bitcast_fusion), channel_id=1, replica_groups=mesh['grp'=2,'pencil'=4,'depth'=2,'mem'=2] {'pencil'}, dimensions={0} | all-to-all | bytes 8388608 | tf_op jit(solution)/shard_map/all_to_all | solution.py:176
  705.0 5.3 copy.110
  (38 shorter events, 73.6 us)
Async XLA Ops:
  6.5 549.2 %all-reduce.2.cloned.1.call-start = ((), (), s32[]{:S(2)}) async-start(), calls=%async_computation.1 | async-start | bytes 16777216 | tf_op jit(solution)/shard_map/psum | solution.py:167
  57.6 52.0 %collective-permute-start.2 = (f32[1,2,512,512]{3,2,1,0:T(8,128)}, f32[1,2,512,512]{3,2,1,0:T(8,128)}, u32[]{:S(2)}, u32[]{:S(2)}) collective-permute-start(f32[1,2,512,512]{3,2,1,0:T(8,128)} %bitcast.243), channel_id=1, source_target_pairs={{0,12},{4,8},{8,4},{12,0},{1,13},{5,9},{9,5},{13,1},{2,14},{6,10},... | collective-permute-start | bytes 6291464 | tf_op jit(solution)/shard_map/ppermute | solution.py:145
  65.5 177.0 %collective-permute-start.1 = (f32[1,2,512,512]{3,2,1,0:T(8,128)}, f32[1,2,512,512]{3,2,1,0:T(8,128)}, u32[]{:S(2)}, u32[]{:S(2)}) collective-permute-start(f32[1,2,512,512]{3,2,1,0:T(8,128)} %bitcast.244), channel_id=1, source_target_pairs={{0,8},{4,12},{8,0},{12,4},{1,9},{5,13},{9,1},{13,5},{2,10},{6,14},... | collective-permute-start | bytes 6291464 | tf_op jit(solution)/shard_map/ppermute | solution.py:145
  68.5 174.1 %collective-permute-start = (f32[1,2,512,512]{3,2,1,0:T(8,128)}, f32[1,2,512,512]{3,2,1,0:T(8,128)}, u32[]{:S(2)}, u32[]{:S(2)}) collective-permute-start(f32[1,2,512,512]{3,2,1,0:T(8,128)} %bitcast.245), channel_id=1, source_target_pairs={{0,4},{4,0},{8,12},{12,8},{1,5},{5,1},{9,13},{13,9},{2,6},{6,2},{1... | collective-permute-start | bytes 6291464 | tf_op jit(solution)/shard_map/ppermute | solution.py:145
  71.7 170.9 %copy-start = (f32[1,2,512,1,512]{4,2,1,3,0:T(8,128)S(1)}, f32[1,2,512,1,512]{4,2,1,3,0:T(8,128)}, u32[]{:S(2)}) copy-start(f32[1,2,512,1,512]{4,2,1,3,0:T(8,128)} %copy.80) | copy-start | bytes 6291460
Sparse Core Ops, SparseCore 0:
  357.6 198.1 all-reduce.1
